TPU v7x, 512 devices: a whole 4x8x8 slice. The times are simulated.
512 devices in a mesh: grp: 8 (over z_lo, core), blk: 64 (over y, x, z_hi).
Axes of the slice: x: 4, y: 8, z: 8 (z_hi: 2, z_lo: 4; z = z_hi * 4 + z_lo), core: 2. Of those that a mesh axis runs over, the one named last changes fastest.
Arguments:
- images: bfloat16 [196608, 1152], P(('grp', 'blk')), may hold values from -1 to 1
- texts: bfloat16 [196608, 1152], P(('grp', 'blk')), may hold values from -1 to 1
- row_pair_labels: int32 [196608], P(('grp', 'blk')), may hold values from 0 to 1535
- logit_scale_log: float32 [1], replicated, may hold values from -0.7 to 0.7
- logit_bias: float32 [1], replicated, may hold values from -3 to 0
Outputs:
- row_loss: float32 [196608], P(('grp', 'blk'))
- image_embed_gradient: bfloat16 [196608, 1152], P(('grp', 'blk'))
- text_embed_gradient: bfloat16 [196608, 1152], P(('grp', 'blk'))
All inputs are finite; a program needn't handle non-finite values.
Results may differ from a plain program's by a relative error of at most 0.0049.
Values may be sent and summed in bfloat16 or wider, within the bound.
A program may use at most 64 MiB of HBM per device.

v0:
```python
import jax
import jax.numpy as jnp
from jax import lax
from jax.sharding import PartitionSpec as P


def passed_along(value, axis, steps):
    count = lax.axis_size(axis)
    pairs = [(source, (source + steps) % count) for source in range(count)]
    return lax.ppermute(value, axis, pairs)


def build_pair_logits(
    image_block_rows,
    image_pair_labels,
    text_block_rows,
    text_pair_labels,
    logit_multiplier,
    block_shift,
):
    pair_logits = (
        logit_multiplier
        * lax.dot_general(
            image_block_rows,
            text_block_rows,
            (((1,), (1,)), ((), ())),
            preferred_element_type=jnp.float32,
        )
        + block_shift
    )
    positive_match = (image_pair_labels[:, None] == text_pair_labels[None, :]).astype(jnp.float32)
    return (pair_logits, positive_match)


def block_loss_terms(
    image_block_rows,
    image_pair_labels,
    text_block_rows,
    text_pair_labels,
    logit_multiplier,
    block_shift,
):
    pair_logits, positive_match = build_pair_logits(
        image_block_rows,
        image_pair_labels,
        text_block_rows,
        text_pair_labels,
        logit_multiplier,
        block_shift,
    )
    row_sum = jnp.sum(jax.nn.softplus(pair_logits) - positive_match * pair_logits, axis=1)
    coefficient = (jax.nn.sigmoid(pair_logits) - positive_match).astype(jnp.bfloat16)
    image_part = jnp.dot(coefficient, text_block_rows, preferred_element_type=jnp.float32)
    text_part = lax.dot_general(
        coefficient, image_block_rows, (((0,), (0,)), ((), ())), preferred_element_type=jnp.float32
    )
    return (row_sum, image_part, text_part)


def per_device(images, texts, row_pair_labels, logit_scale_log, logit_bias):
    logit_multiplier = jnp.exp(logit_scale_log[0])
    block_shift = logit_bias[0]
    row_sum, image_gradient_sum, own_part = block_loss_terms(
        images, row_pair_labels, texts, row_pair_labels, logit_multiplier, block_shift
    )
    shifted_texts, shifted_pair_ids = passed_along((texts, row_pair_labels), "grp", 1)
    rotating_texts, rotating_pair_ids = (texts, row_pair_labels)
    carried = own_part
    for visit in range(2):
        rotating_texts, rotating_pair_ids = passed_along(
            (rotating_texts, rotating_pair_ids), "blk", 1
        )
        loss_part, image_part, text_part = block_loss_terms(
            images,
            row_pair_labels,
            rotating_texts,
            rotating_pair_ids,
            logit_multiplier,
            block_shift,
        )
        carried = passed_along(carried, "blk", 1) + text_part
        row_sum = row_sum + loss_part
        image_gradient_sum = image_gradient_sum + image_part
    loss_part, image_part, hop_part = block_loss_terms(
        images, row_pair_labels, shifted_texts, shifted_pair_ids, logit_multiplier, block_shift
    )
    row_sum = row_sum + loss_part
    image_gradient_sum = image_gradient_sum + image_part
    returned = passed_along(hop_part, "grp", -1)
    text_gradient_sum = passed_along(carried, "blk", -2) + returned
    row_loss = row_sum / (4 * images.shape[0])
    image_embed_gradient = (logit_multiplier * image_gradient_sum).astype(jnp.bfloat16)
    text_embed_gradient = (logit_multiplier * text_gradient_sum).astype(jnp.bfloat16)
    return (row_loss, image_embed_gradient, text_embed_gradient)


def solution(mesh):
    in_specs = (P(("grp", "blk"), None), P(("grp", "blk"), None), P(("grp", "blk")), P(), P())
    out_specs = (P(("grp", "blk")), P(("grp", "blk"), None), P(("grp", "blk"), None))
    return jax.shard_map(
        per_device, mesh=mesh, in_specs=in_specs, out_specs=out_specs, check_vma=False
    )
```

profile of v0, /device:TPU:129, one launch (start us, length us, event | category | flops | bytes accessed | tf_op | source)
XLA Modules:
  0.0 328.2 jit_solution(12432749407186705294)
XLA Ops:
  0.6 0.0 copy-start
  0.7 9.0 %collective-permute-start = (bf16[384,1152]{1,0:T(8,128)(2,1)}, bf16[384,1152]{1,0:T(8,128)(2,1)S(1)}, u32[]{:S(2)}, u32[]{:S(2)}) collective-permute-start(bf16[384,1152]{1,0:T(8,128)(2,1)} %param.6), channel_id=1, source_target_pairs={{0,1},{1,2},{2,3},{3,4},{4,5},{5,6},{6,7},{7,8},{8,9},{9,10},{10,1... | collective-permute-start | bytes 2654216 | tf_op jit(solution)/shard_map/ppermute | solution.py:10
  9.6 3.9 %collective-permute-start.4 = (bf16[384,1152]{1,0:T(8,128)(2,1)}, bf16[384,1152]{1,0:T(8,128)(2,1)S(1)}, u32[]{:S(2)}, u32[]{:S(2)}) collective-permute-start(bf16[384,1152]{1,0:T(8,128)(2,1)} %param.6), channel_id=1, source_target_pairs={{0,64},{64,128},{128,192},{192,256},{256,320},{320,384},{384,448},... | collective-permute-start | bytes 2654216 | tf_op jit(solution)/shard_map/ppermute | solution.py:10
  14.9 1.8 fusion.6
  16.8 0.7 fusion.23
  17.5 2.2 collective-permute-start.6
  19.7 33.7 %collective-permute-done = bf16[384,1152]{1,0:T(8,128)(2,1)S(1)} collective-permute-done((bf16[384,1152]{1,0:T(8,128)(2,1)}, bf16[384,1152]{1,0:T(8,128)(2,1)S(1)}, u32[]{:S(2)}, u32[]{:S(2)}) %collective-permute-start) | collective-permute-done | bytes 884768 | tf_op jit(solution)/shard_map/ppermute | solution.py:10
  53.4 3.2 collective-permute-start.2
  56.6 4.7 %collective-permute-start.1 = (s32[384]{0:T(512)S(1)}, s32[384]{0:T(512)S(1)}, u32[]{:S(2)}, u32[]{:S(2)}) collective-permute-start(s32[384]{0:T(512)S(1)} %copy-done.1), channel_id=1, source_target_pairs={{0,1},{1,2},{2,3},{3,4},{4,5},{5,6},{6,7},{7,8},{8,9},{9,10},{10,1... | collective-permute-start | bytes 4616 | tf_op jit(solution)/shard_map/ppermute | solution.py:10
  61.3 3.7 %collective-permute-start.5 = (s32[384]{0:T(512)S(1)}, s32[384]{0:T(512)S(1)}, u32[]{:S(2)}, u32[]{:S(2)}) collective-permute-start(s32[384]{0:T(512)S(1)} %copy-done.1), channel_id=1, source_target_pairs={{0,64},{64,128},{128,192},{192,256},{256,320},{320,384},{384,448},... | collective-permute-start | bytes 4616 | tf_op jit(solution)/shard_map/ppermute | solution.py:10
  65.0 106.4 %collective-permute-done.1 = s32[384]{0:T(512)S(1)} collective-permute-done((s32[384]{0:T(512)S(1)}, s32[384]{0:T(512)S(1)}, u32[]{:S(2)}, u32[]{:S(2)}) %collective-permute-start.1) | collective-permute-done | bytes 1568 | tf_op jit(solution)/shard_map/ppermute | solution.py:10
  171.4 7.7 %collective-permute-start.3 = (s32[384]{0:T(512)S(1)}, s32[384]{0:T(512)S(1)}, u32[]{:S(2)}, u32[]{:S(2)}) collective-permute-start(s32[384]{0:T(512)S(1)} %collective-permute-done.1), channel_id=1, source_target_pairs={{0,1},{1,2},{2,3},{3,4},{4,5},{5,6},{6,7},{7,8},{8,9},{9,10},{10,1... | collective-permute-start | bytes 4616 | tf_op jit(solution)/shard_map/ppermute | solution.py:10
  179.1 0.0 collective-permute-done.4
  179.1 0.7 fusion.3
  179.8 0.7 fusion.4
  180.4 5.4 %collective-permute-done.3 = s32[384]{0:T(512)S(1)} collective-permute-done((s32[384]{0:T(512)S(1)}, s32[384]{0:T(512)S(1)}, u32[]{:S(2)}, u32[]{:S(2)}) %collective-permute-start.3) | collective-permute-done | bytes 1568 | tf_op jit(solution)/shard_map/ppermute | solution.py:10
  185.9 2.0 fusion.12
  187.8 0.8 convolution_add_fusion
  188.6 1.9 collective-permute-start.7
  190.5 0.7 fusion.27
  191.3 0.0 copy-start.2
  191.3 2.1 collective-permute-start.9
  193.4 86.5 %collective-permute-done.7 = f32[384,1152]{1,0:T(8,128)S(1)} collective-permute-done((f32[384,1152]{1,0:T(8,128)S(1)}, f32[384,1152]{1,0:T(8,128)S(1)}, u32[]{:S(2)}, u32[]{:S(2)}) %collective-permute-start.7) | collective-permute-done | bytes 1769504 | tf_op jit(solution)/shard_map/ppermute | solution.py:10
  279.8 0.8 fusion.34
  280.6 8.5 %collective-permute-start.8 = (f32[384,1152]{1,0:T(8,128)S(1)}, f32[384,1152]{1,0:T(8,128)S(1)}, u32[]{:S(2)}, u32[]{:S(2)}) collective-permute-start(f32[384,1152]{1,0:T(8,128)S(1)} %fusion.34), channel_id=1, source_target_pairs={{0,62},{1,63},{2,0},{3,1},{4,2},{5,3},{6,4},{7,5},{8,6},{9,7},{10,... | collective-permute-start | bytes 5308424 | tf_op jit(solution)/shard_map/ppermute | solution.py:10
  289.1 0.8 fusion.25
  289.9 0.8 fusion.29
  290.7 0.6 add_multiply_fusion
  291.3 0.8 convolution_add_fusion.2
  292.1 1.7 fusion.2
  293.8 33.3 %collective-permute-done.8 = f32[384,1152]{1,0:T(8,128)S(1)} collective-permute-done((f32[384,1152]{1,0:T(8,128)S(1)}, f32[384,1152]{1,0:T(8,128)S(1)}, u32[]{:S(2)}, u32[]{:S(2)}) %collective-permute-start.8) | collective-permute-done | bytes 1769504 | tf_op jit(solution)/shard_map/ppermute | solution.py:10
  327.1 1.1 multiply_convert_fusion
  (8 shorter events, 0.0 us)
Async XLA Ops:
  0.6 14.3 %copy-start = (bf16[384,1152]{1,0:T(8,128)(2,1)S(1)}, bf16[384,1152]{1,0:T(8,128)(2,1)}, u32[]{:S(2)}) copy-start(bf16[384,1152]{1,0:T(8,128)(2,1)} %param.5) | copy-start | bytes 2654212
  0.6 16.1 %copy-start.1 = (s32[384]{0:T(512)S(1)}, s32[384]{0:T(512)}, u32[]{:S(2)}) copy-start(s32[384]{0:T(512)} %param.7) | copy-start | bytes 4612
  0.7 52.8 %collective-permute-start = (bf16[384,1152]{1,0:T(8,128)(2,1)}, bf16[384,1152]{1,0:T(8,128)(2,1)S(1)}, u32[]{:S(2)}, u32[]{:S(2)}) collective-permute-start(bf16[384,1152]{1,0:T(8,128)(2,1)} %param.6), channel_id=1, source_target_pairs={{0,1},{1,2},{2,3},{3,4},{4,5},{5,6},{6,7},{7,8},{8,9},{9,10},{10,1... | collective-permute-start | bytes 2654216 | tf_op jit(solution)/shard_map/ppermute | solution.py:10
  9.6 169.4 %collective-permute-start.4 = (bf16[384,1152]{1,0:T(8,128)(2,1)}, bf16[384,1152]{1,0:T(8,128)(2,1)S(1)}, u32[]{:S(2)}, u32[]{:S(2)}) collective-permute-start(bf16[384,1152]{1,0:T(8,128)(2,1)} %param.6), channel_id=1, source_target_pairs={{0,64},{64,128},{128,192},{192,256},{256,320},{320,384},{384,448},... | collective-permute-start | bytes 2654216 | tf_op jit(solution)/shard_map/ppermute | solution.py:10
  17.5 170.3 %collective-permute-start.6 = (f32[384,1152]{1,0:T(8,128)S(1)}, f32[384,1152]{1,0:T(8,128)S(1)}, u32[]{:S(2)}, u32[]{:S(2)}) collective-permute-start(f32[384,1152]{1,0:T(8,128)S(1)} %fusion.23), channel_id=1, source_target_pairs={{0,1},{1,2},{2,3},{3,4},{4,5},{5,6},{6,7},{7,8},{8,9},{9,10},{10,1... | collective-permute-start | bytes 5308424 | tf_op jit(solution)/shard_map/ppermute | solution.py:10
  53.4 126.3 %collective-permute-start.2 = (bf16[384,1152]{1,0:T(8,128)(2,1)S(1)}, bf16[384,1152]{1,0:T(8,128)(2,1)S(1)}, u32[]{:S(2)}, u32[]{:S(2)}) collective-permute-start(bf16[384,1152]{1,0:T(8,128)(2,1)S(1)} %collective-permute-done), channel_id=1, source_target_pairs={{0,1},{1,2},{2,3},{3,4},{4,5},{5,6},{6,7},{7,8},{8,9},{9,10},{10,1... | collective-permute-start | bytes 2654216 | tf_op jit(solution)/shard_map/ppermute | solution.py:10
  56.6 114.8 %collective-permute-start.1 = (s32[384]{0:T(512)S(1)}, s32[384]{0:T(512)S(1)}, u32[]{:S(2)}, u32[]{:S(2)}) collective-permute-start(s32[384]{0:T(512)S(1)} %copy-done.1), channel_id=1, source_target_pairs={{0,1},{1,2},{2,3},{3,4},{4,5},{5,6},{6,7},{7,8},{8,9},{9,10},{10,1... | collective-permute-start | bytes 4616 | tf_op jit(solution)/shard_map/ppermute | solution.py:10
  61.3 119.1 %collective-permute-start.5 = (s32[384]{0:T(512)S(1)}, s32[384]{0:T(512)S(1)}, u32[]{:S(2)}, u32[]{:S(2)}) collective-permute-start(s32[384]{0:T(512)S(1)} %copy-done.1), channel_id=1, source_target_pairs={{0,64},{64,128},{128,192},{192,256},{256,320},{320,384},{384,448},... | collective-permute-start | bytes 4616 | tf_op jit(solution)/shard_map/ppermute | solution.py:10
  171.4 14.5 %collective-permute-start.3 = (s32[384]{0:T(512)S(1)}, s32[384]{0:T(512)S(1)}, u32[]{:S(2)}, u32[]{:S(2)}) collective-permute-start(s32[384]{0:T(512)S(1)} %collective-permute-done.1), channel_id=1, source_target_pairs={{0,1},{1,2},{2,3},{3,4},{4,5},{5,6},{6,7},{7,8},{8,9},{9,10},{10,1... | collective-permute-start | bytes 4616 | tf_op jit(solution)/shard_map/ppermute | solution.py:10
  188.6 91.2 %collective-permute-start.7 = (f32[384,1152]{1,0:T(8,128)S(1)}, f32[384,1152]{1,0:T(8,128)S(1)}, u32[]{:S(2)}, u32[]{:S(2)}) collective-permute-start(f32[384,1152]{1,0:T(8,128)S(1)} %convolution_add_fusion), channel_id=1, source_target_pairs={{0,1},{1,2},{2,3},{3,4},{4,5},{5,6},{6,7},{7,8},{8,9},{9,10},{10,1... | collective-permute-start | bytes 5308424 | tf_op jit(solution)/shard_map/ppermute | solution.py:10
  191.3 97.8 %copy-start.2 = (bf16[384,1152]{1,0:T(8,128)(2,1)S(1)}, bf16[384,1152]{1,0:T(8,128)(2,1)}, u32[]{:S(2)}) copy-start(bf16[384,1152]{1,0:T(8,128)(2,1)} %param.6) | copy-start | bytes 2654212
  191.3 102.5 %collective-permute-start.9 = (f32[384,1152]{1,0:T(8,128)S(1)}, f32[384,1152]{1,0:T(8,128)S(1)}, u32[]{:S(2)}, u32[]{:S(2)}) collective-permute-start(f32[384,1152]{1,0:T(8,128)S(1)} %fusion.27), channel_id=1, source_target_pairs={{0,448},{64,0},{128,64},{192,128},{256,192},{320,256},{384,320},{4... | collective-permute-start | bytes 5308424 | tf_op jit(solution)/shard_map/ppermute | solution.py:10
  280.6 46.5 %collective-permute-start.8 = (f32[384,1152]{1,0:T(8,128)S(1)}, f32[384,1152]{1,0:T(8,128)S(1)}, u32[]{:S(2)}, u32[]{:S(2)}) collective-permute-start(f32[384,1152]{1,0:T(8,128)S(1)} %fusion.34), channel_id=1, source_target_pairs={{0,62},{1,63},{2,0},{3,1},{4,2},{5,3},{6,4},{7,5},{8,6},{9,7},{10,... | collective-permute-start | bytes 5308424 | tf_op jit(solution)/shard_map/ppermute | solution.py:10
where the time goes:
time: 329 us; the launch traced here: 328 us
  waiting for transfers between devices  265 us (81%)
  starting transfers between devices  46.8 us (14%)
  matrix products  12.2 us (4%)
    ppermute x10, waiting for transfers between devices, passed_along(): return lax.ppermute(value, axis, pairs)  265 us
    ppermute x10, starting transfers between devices, passed_along(): return lax.ppermute(value, axis, pairs)  46.8 us
  transfers between devices with their start and end apart: 10, of which 5 were waited for; matrix products, arithmetic and copies ran while one was open for 4% of the time, Pallas kernels for 0%

commit v1 on v0

v1 whole, which is shorter than its diff:
```python
import functools
import jax
import jax.numpy as jnp
from jax import lax
from jax.experimental import pallas as pl
from jax.experimental.pallas import tpu as pltpu
from jax.sharding import PartitionSpec as P

MESH = pl.DeviceIdType.MESH
ROWS = 128


def kernel(
    groups, blocks, cfg,
    scale_ref, bias_ref, labels_ref, images_ref, texts_ref,
    loss_ref, image_out, text_out,
    held, labels, columns, total, losses,
    load_sem, send_sem, recv_sem, label_send, label_recv,
):
    g, k = lax.axis_index("grp"), lax.axis_index("blk")
    odd = lax.rem(g, 2)
    SR = cfg["send_rows"]
    chunks = held.shape[1] // ROWS
    pieces = held.shape[1] // SR
    lows = groups // 2
    deep = 2 * lows

    def at(dg, dk):
        return (lax.rem(g + dg + groups, groups), lax.rem(k + dk + blocks, blocks))

    def world(w, place):
        return (place[0] + w * (groups - 1 - 2 * place[0]), place[1] + w * (blocks - 1 - 2 * place[1]))

    def height(place):
        return lows * lax.rem(place[1], 2) + place[0] // 2

    def on_chip(z, core, place):
        z = lax.rem(z + 2 * deep, deep)
        return (2 * lax.rem(z, lows) + core, place[1] - lax.rem(place[1], 2) + z // lows)

    def inner(z):
        return jnp.where(lax.rem(z + 2 * deep, lows) < lows - 1, 1, 0)

    def way(place):
        return jnp.where(lax.rem(place[0], 2) == inner(place[0] // 2), 0, 1)

    def core_of(z, down):
        return inner(z) + down * (1 - 2 * inner(z))

    mine = world(odd, (g, k))
    z = height(mine)

    def passes_to(down):
        return world(odd, on_chip(z + 1 - 2 * down, 0, mine))

    def taken_from(down):
        source = z - 1 + 2 * down
        return world(odd, on_chip(source, core_of(source, down), mine))

    def ends_at(down):
        source = z - (lows - 1) * (1 - 2 * down)
        start = on_chip(source, core_of(source, down), mine)
        return world(odd, (start[0], lax.rem(start[1] + 1, blocks)))

    def first_to(w):
        place = world(w, (g, k))
        down = way(place)
        return world(w, on_chip(height(place) + 1 - 2 * down, 0, place)), down

    def last_from(w):
        place = world(w, (g, k))
        source = (place[0], lax.rem(place[1] + blocks - 1, blocks))
        down = way(source)
        return world(w, on_chip(height(source) + (lows - 1) * (1 - 2 * down), 0, source))

    targets = [at(0, 1), at(0, 2), at(1, 0), at(0, -1), at(0, -2), at(-1, 0)]
    text_first, text_down = first_to(0)
    image_first, image_down = first_to(1)
    peers = targets + [
        passes_to(0), passes_to(1), taken_from(0), taken_from(1), ends_at(0), ends_at(1),
        text_first, image_first, last_from(0), last_from(1),
    ]
    barrier = pltpu.get_barrier_semaphore()
    for peer in peers:
        pl.semaphore_signal(barrier, inc=1, device_id=peer, device_id_type=MESH)
    loads = [
        pltpu.make_async_copy(texts_ref, held.at[6], load_sem.at[0]),
        pltpu.make_async_copy(images_ref, held.at[7], load_sem.at[1]),
    ]
    for load in loads:
        load.start()
    labels[6, 0:chunks] = labels_ref[...]
    labels[7, 0:chunks] = labels_ref[...]
    pl.semaphore_wait(barrier, len(peers))

    def block_copy(source, slot, piece, flow, device):
        rows = pl.ds(pl.multiple_of(piece * SR, SR), SR)
        return pltpu.make_async_remote_copy(
            src_ref=source.at[rows], dst_ref=held.at[slot, rows],
            send_sem=send_sem.at[flow, piece], recv_sem=recv_sem.at[slot, piece],
            device_id=device, device_id_type=MESH,
        )

    def first(w, piece):
        if w == 0:
            return block_copy(texts_ref, 8 + 3 * text_down, piece, 0, text_first)
        return block_copy(images_ref, 8 + 3 * image_down, piece, 1, image_first)

    def along(w, piece):
        if w == 0:
            return block_copy(texts_ref, 1, piece, 2, targets[1])
        return block_copy(images_ref, 4, piece, 3, targets[4])

    partner = (g + 1 - 2 * odd, k)

    def beside(piece):
        return block_copy(held.at[6 + odd], 2 + 3 * odd, piece, 4, partner)

    def onward(down, hop, piece):
        buffer = 7 + 3 * down + hop
        end = ends_at(down)
        step_to = passes_to(down)
        final = hop == 3
        slot = jnp.where(final, 3 * odd, buffer + 1)
        device = (jnp.where(final, end[0], step_to[0]), jnp.where(final, end[1], step_to[1]))
        return block_copy(held.at[buffer], slot, piece, 4 + 3 * down + hop, device)

    label_copies = [
        pltpu.make_async_remote_copy(
            src_ref=labels.at[6], dst_ref=labels.at[slot],
            send_sem=label_send.at[slot], recv_sem=label_recv.at[slot],
            device_id=targets[slot], device_id_type=MESH,
        )
        for slot in range(6)
    ]

    for piece in range(pieces):
        first(0, piece).start()
        first(1, piece).start()
    for copy in label_copies:
        copy.start()
    for piece in range(pieces):
        along(0, piece).start()
        along(1, piece).start()
    for load in loads:
        load.wait()
    for piece in range(pieces):
        beside(piece).start()

    t = jnp.exp(jnp.full((1, ROWS), scale_ref[0], jnp.float32))
    b = bias_ref[0]
    for c in range(chunks):
        row = labels_ref[c : c + 1, :].astype(jnp.float32)
        columns[c * ROWS : (c + 1) * ROWS] = jnp.transpose(jnp.broadcast_to(row, (ROWS, ROWS)))
    total[...] = jnp.zeros_like(total)
    losses[...] = jnp.zeros_like(losses)

    def step(side, buffer, slot, chunk):
        rows = pl.ds(pl.multiple_of(chunk * ROWS, ROWS), ROWS)
        moving = held[buffer, rows]
        logit = t * lax.dot_general(
            held[7 - side], moving, (((1,), (1,)), ((), ())), preferred_element_type=jnp.float32
        ) + b
        match = columns[...] == labels[slot, pl.ds(chunk, 1)].astype(jnp.float32)
        small = jnp.exp(-jnp.abs(logit))
        loss = jnp.maximum(logit, 0.0) + jnp.log1p(small) - jnp.where(match, logit, 0.0)
        gate = jnp.where(logit >= 0.0, 1.0, small) / (1.0 + small)
        coefficient = (gate - jnp.where(match, 1.0, 0.0)).astype(jnp.bfloat16)
        losses[side] += loss
        total[side] += jnp.dot(coefficient, moving, preferred_element_type=jnp.float32)

    def arrive(slot, piece):
        rows = pl.ds(pl.multiple_of(piece * SR, SR), SR)
        pltpu.make_async_copy(held.at[slot, rows], held.at[slot, rows], recv_sem.at[slot, piece]).wait()

    def arrive_rows(slot, chunk):
        for q in range(ROWS // SR):
            arrive(slot, chunk * (ROWS // SR) + q)

    def pass_on(hop, chunk):
        for q in range(ROWS // SR):
            for down in range(2):
                piece = chunk * (ROWS // SR) + q
                arrive(7 + 3 * down + hop, piece)
                onward(down, hop, piece).start()

    near = 5 - 3 * odd
    nearby = 8 + jnp.where(mine[0] == 0, 5, 0)

    def labels_arrive(slot):
        pltpu.make_async_copy(labels.at[slot], labels.at[slot], label_recv.at[slot]).wait()

    for slot in range(6):
        labels_arrive(slot)

    def rounds(n, carry):
        hop, chunk = n // chunks + 1, lax.rem(n, chunks)
        pass_on(hop, chunk)

        @pl.when(hop == 2)
        def _():
            arrive_rows(near, chunk)
            arrive_rows(1, chunk)

        @pl.when(hop == 3)
        def _():
            arrive_rows(4, chunk)

        if cfg["compute"]:
            buffer_a = jnp.where(hop == 1, 6, jnp.where(hop == 2, near, 4))
            side_a = jnp.where(hop == 1, 0, jnp.where(hop == 2, 1 - odd, 1))
            buffer_b = jnp.where(hop == 1, 7, jnp.where(hop == 2, 1, nearby))
            side_b = jnp.where(hop == 1, 1, jnp.where(hop == 2, 0, odd))
            slot_b = jnp.where(hop == 3, 2 + 3 * odd, buffer_b)

            def pair(i, carry):
                step(
                    jnp.where(i == 0, side_a, side_b), jnp.where(i == 0, buffer_a, buffer_b),
                    jnp.where(i == 0, buffer_a, slot_b), chunk,
                )
                return carry

            lax.fori_loop(0, 2, pair, 0)
        return carry

    lax.fori_loop(0, 3 * chunks, rounds, 0)

    def ends(n, carry):
        slot, chunk = 3 * lax.rem(n, 2), n // 2
        arrive_rows(slot, chunk)
        if cfg["compute"]:
            step(lax.rem(n, 2), slot, slot, chunk)
        return carry

    lax.fori_loop(0, 2 * chunks, ends, 0)

    for side, out in ((0, image_out), (1, text_out)):
        out[...] = (jnp.tile(t, (1, out.shape[1] // ROWS)) * total[side]).astype(jnp.bfloat16)
    for c in range(chunks):
        part = losses[0, c * ROWS : (c + 1) * ROWS]
        loss_ref[c : c + 1, :] = jnp.sum(jnp.transpose(part), axis=0, keepdims=True) * (
            1.0 / (4 * held.shape[1])
        )
    for copy in label_copies:
        copy.wait_send()
    for piece in range(pieces):
        first(0, piece).wait_send()
        first(1, piece).wait_send()
        along(0, piece).wait_send()
        along(1, piece).wait_send()
        beside(piece).wait_send()
        for down in range(2):
            for hop in (1, 2, 3):
                onward(down, hop, piece).wait_send()


def per_device(groups, blocks, cfg, images, texts, row_pair_labels, logit_scale_log, logit_bias):
    rows, width = images.shape
    chunks = rows // ROWS
    pieces = rows // cfg["send_rows"]
    vmem = pl.BlockSpec(memory_space=pltpu.VMEM)
    anywhere = pl.BlockSpec(memory_space=pl.ANY)
    smem = pl.BlockSpec(memory_space=pltpu.SMEM)
    loss, image_grad, text_grad = pl.pallas_call(
        functools.partial(kernel, groups, blocks, cfg),
        out_shape=(
            jax.ShapeDtypeStruct((chunks, ROWS), jnp.float32),
            jax.ShapeDtypeStruct((rows, width), jnp.bfloat16),
            jax.ShapeDtypeStruct((rows, width), jnp.bfloat16),
        ),
        in_specs=[smem, smem, vmem, anywhere, anywhere],
        out_specs=(vmem, vmem, vmem),
        scratch_shapes=[
            pltpu.VMEM((14, rows, width), jnp.bfloat16),
            pltpu.VMEM((8, 8, ROWS), jnp.int32),
            pltpu.VMEM((rows, ROWS), jnp.float32),
            pltpu.VMEM((2, rows, width), jnp.float32),
            pltpu.VMEM((2, rows, ROWS), jnp.float32),
            pltpu.SemaphoreType.DMA((2,)),
            pltpu.SemaphoreType.DMA((11, pieces)),
            pltpu.SemaphoreType.DMA((14, pieces)),
            pltpu.SemaphoreType.DMA((6,)),
            pltpu.SemaphoreType.DMA((6,)),
        ],
        compiler_params=pltpu.CompilerParams(
            collective_id=cfg.get("id", 0), has_side_effects=True, vmem_limit_bytes=60 << 20
        ),
        cost_estimate=pl.CostEstimate(
            flops=32 * rows * rows * width, bytes_accessed=8 * rows * width, transcendentals=24 * rows * rows
        ),
        name=cfg.get("name"),
    )(logit_scale_log, logit_bias, row_pair_labels.reshape(chunks, ROWS), images, texts)
    return loss.reshape(rows), image_grad, text_grad

CFG = {"compute": True, "send_rows": 128}

def solution(mesh):
    groups, blocks = mesh.shape["grp"], mesh.shape["blk"]
    both = P(("grp", "blk"))
    wide = P(("grp", "blk"), None)
    return jax.shard_map(
        functools.partial(per_device, groups, blocks, CFG),
        mesh=mesh,
        in_specs=(wide, wide, both, P(), P()),
        out_specs=(both, wide, wide),
        check_vma=False,
    )
```

time: 329 us -> 110 us (0.33)
  the two profiles are of different devices: /device:TPU:129 before, /device:TPU:1 now
where the time goes in v1:
time: 110 us; the launch traced here: 108 us
  Pallas kernels  101 us (92%)
  local copies, waits for them, and re-layouts  4.39 us (4%)
  between operations  1.94 us (2%)
    pallas_call x1, Pallas kernels, per_device(): pl.pallas_call(functools.partial(kernel, groups, blocks, cfg), out_shape=...  101 us
    unnamed x7, local copies, waits for them, and re-layouts  4.39 us

profile of v1, /device:TPU:1, one launch (start us, length us, event | category | flops | bytes accessed | tf_op | source)
XLA Modules:
  0.0 107.6 jit_solution(11398116834243764444)
XLA Ops:
  1.9 101.3 %shard_map.76 = (f32[3,128]{1,0:T(4,128)}, bf16[384,1152]{1,0:T(8,128)(2,1)}, bf16[384,1152]{1,0:T(8,128)(2,1)}) custom-call(f32[1]{0:T(128)S(6)} %copy.11.scale_ref, f32[1]{0:T(128)S(6)} %copy.12.bias_ref, s32[3,128]{1,0:T(4,128)} %bitcast.3, bf16[384,1152]{1,0:T(8,128)(2,1)} %images_ref.1, bf16[384,1152]{1,0:T(8,128)(2,1)} %texts_ref.1), custom_call_target="tpu_custom_call" | custom-call | flops 5435817984 | bytes 3538944 | tf_op jit(solution)/shard_map/pallas_call | solution.py:264
  103.2 0.0 copy-start.1
  103.2 0.7 copy-done.1
  103.9 0.6 copy.13
  104.5 0.0 copy-start
  104.5 2.2 %copy.14 = bf16[384,1152]{1,0:T(8,128)(2,1)} copy(bf16[384,1152]{1,0:T(8,128)(2,1)} %get-tuple-element.13) | data formatting | bytes 1769472
  106.7 0.0 copy-done
  106.7 0.9 copy.15
Async XLA Ops:
  103.2 0.7 copy-start.1
  104.5 2.2 %copy-start = (bf16[384,1152]{1,0:T(8,128)(2,1)S(1)}, bf16[384,1152]{1,0:T(8,128)(2,1)}, u32[]{:S(2)}) copy-start(bf16[384,1152]{1,0:T(8,128)(2,1)} %get-tuple-element.14) | copy-start | bytes 2654212

commit v2 on v1

v2 whole, which is shorter than its diff:
```python
import functools
import jax
import jax.numpy as jnp
from jax import lax
from jax.experimental import pallas as pl
from jax.experimental.pallas import tpu as pltpu
from jax.sharding import PartitionSpec as P

MESH = pl.DeviceIdType.MESH
ROWS = 128
SEND = 128


def kernel(
    groups, blocks,
    scale_in, bias_in, labels_in, images_ref, texts_ref,
    loss_ref, image_out, text_out,
    held, labels, columns, total, losses, scale_ref, bias_ref,
    load_sem, send_sem, recv_sem, label_send, label_recv, ready,
):
    g, k = lax.axis_index("grp"), lax.axis_index("blk")
    odd = lax.rem(g, 2)
    chunks = held.shape[1] // ROWS
    pieces = held.shape[1] // SEND
    lows = groups // 2
    deep = 2 * lows

    def at(dg, dk):
        return (lax.rem(g + dg + groups, groups), lax.rem(k + dk + blocks, blocks))

    def world(w, place):
        return (place[0] + w * (groups - 1 - 2 * place[0]), place[1] + w * (blocks - 1 - 2 * place[1]))

    def height(place):
        return lows * lax.rem(place[1], 2) + place[0] // 2

    def on_chip(z, core, place):
        z = lax.rem(z + 2 * deep, deep)
        return (2 * lax.rem(z, lows) + core, place[1] - lax.rem(place[1], 2) + z // lows)

    def inner(z):
        return jnp.where(lax.rem(z + 2 * deep, lows) < lows - 1, 1, 0)

    def way(place):
        return jnp.where(lax.rem(place[0], 2) == inner(place[0] // 2), 0, 1)

    def core_of(z, down):
        return inner(z) + down * (1 - 2 * inner(z))

    mine = world(odd, (g, k))
    z = height(mine)

    def moved(place, yes):
        return (place[0], lax.rem(place[1] + 2 * yes + blocks, blocks))

    def turns(down, hop, source):
        source = lax.rem(source + 2 * deep, deep)
        if down == 0:
            return jnp.where(hop == 1, source // lows, 0)
        return jnp.where(hop == 3 - inner(source), source // lows, 0)

    def goes_to(down, hop):
        up = 1 - 2 * down
        source = z - hop * up
        core = jnp.where(hop == 3, core_of(source, down), 0)
        return world(odd, moved(on_chip(z + up, core, mine), turns(down, hop, source)))

    def first_to(w):
        place = world(w, (g, k))
        down = way(place)
        return world(w, on_chip(height(place) + 1 - 2 * down, 0, place)), down

    targets = [at(0, 1), at(0, 2), at(1, 0), at(0, -1), at(0, -2), at(-1, 0)]
    text_first, text_down = first_to(0)
    image_first, image_down = first_to(1)
    z_here = height((g, k))
    low = g // 2
    near_z = [on_chip(z_here + 1, 0, (g, k)), on_chip(z_here - 1, 0, (g, k))]
    far = [
        moved(on_chip(z_here + up, 1, (g, k)), side) for side in (-1, 1) for up in (-1, 0, 1)
    ] + [(2 * low + 1, at(0, 1)[1]), (2 * low + 1, at(0, -1)[1]), (2 * (lows - 1 - low) + 1, k)]
    partner = (g + 1 - 2 * odd, k)
    loads = [
        pltpu.make_async_copy(labels_in, labels.at[6], load_sem.at[2]),
        pltpu.make_async_copy(texts_ref, held.at[6], load_sem.at[0]),
        pltpu.make_async_copy(images_ref, held.at[7], load_sem.at[1]),
        pltpu.make_async_copy(scale_in, scale_ref, load_sem.at[3]),
        pltpu.make_async_copy(bias_in, bias_ref, load_sem.at[4]),
        pltpu.make_async_copy(labels_in, labels.at[7], load_sem.at[5]),
    ]
    barrier = pltpu.get_barrier_semaphore()
    for peer in near_z + [partner] + far:
        pl.semaphore_signal(barrier, inc=1, device_id=peer, device_id_type=MESH)
    for load in loads:
        load.start()

    @pl.when(odd == 0)
    def _():
        pl.semaphore_wait(barrier, 2 * len(near_z) + 1)
        pl.semaphore_signal(ready, inc=1, device_id=partner, device_id_type=MESH)

    @pl.when(odd == 1)
    def _():
        pl.semaphore_wait(ready, 1)

    def block_copy(source, slot, piece, flow, device):
        rows = pl.ds(pl.multiple_of(piece * SEND, SEND), SEND)
        return pltpu.make_async_remote_copy(
            src_ref=source.at[rows], dst_ref=held.at[slot, rows],
            send_sem=send_sem.at[flow, piece], recv_sem=recv_sem.at[slot, piece],
            device_id=device, device_id_type=MESH,
        )

    def first(w, piece):
        if w == 0:
            return block_copy(texts_ref, 8 + 3 * text_down, piece, 0, text_first)
        return block_copy(images_ref, 8 + 3 * image_down, piece, 1, image_first)

    def along(w, piece):
        if w == 0:
            return block_copy(texts_ref, 1, piece, 2, targets[1])
        return block_copy(images_ref, 4, piece, 3, targets[4])

    def beside(piece):
        return block_copy(held.at[6 + odd], 2 + 3 * odd, piece, 4, partner)

    def onward(down, hop, piece):
        buffer = 7 + 3 * down + hop
        slot = jnp.where(hop == 3, 3 * odd, buffer + 1)
        return block_copy(held.at[buffer], slot, piece, 4 + 3 * down + hop, goes_to(down, hop))

    label_copies = [
        pltpu.make_async_remote_copy(
            src_ref=labels_in, dst_ref=labels.at[slot],
            send_sem=label_send.at[slot], recv_sem=label_recv.at[slot],
            device_id=targets[slot], device_id_type=MESH,
        )
        for slot in range(6)
    ]

    for piece in range(pieces):
        first(0, piece).start()
        first(1, piece).start()

    @pl.when(odd == 1)
    def _():
        pl.semaphore_wait(barrier, 2 * len(far) + 1)
        pl.semaphore_signal(ready, inc=1, device_id=partner, device_id_type=MESH)

    @pl.when(odd == 0)
    def _():
        pl.semaphore_wait(ready, 1)

    for copy in label_copies:
        copy.start()
    for piece in range(pieces):
        along(0, piece).start()
        along(1, piece).start()
    for load in loads:
        load.wait()
    for piece in range(pieces):
        beside(piece).start()

    t = jnp.exp(jnp.full((1, ROWS), scale_ref[0], jnp.float32))
    b = bias_ref[0]
    for c in range(chunks):
        row = labels[6, c : c + 1, :].astype(jnp.float32)
        columns[c * ROWS : (c + 1) * ROWS] = jnp.transpose(jnp.broadcast_to(row, (ROWS, ROWS)))
    total[...] = jnp.zeros_like(total)
    losses[...] = jnp.zeros_like(losses)

    def step(side, buffer, slot, chunk):
        rows = pl.ds(pl.multiple_of(chunk * ROWS, ROWS), ROWS)
        moving = held[buffer, rows]
        logit = t * lax.dot_general(
            held[7 - side], moving, (((1,), (1,)), ((), ())), preferred_element_type=jnp.float32
        ) + b
        match = columns[...] == labels[slot, pl.ds(chunk, 1)].astype(jnp.float32)
        small = jnp.exp(-jnp.abs(logit))
        loss = jnp.maximum(logit, 0.0) + jnp.log1p(small) - jnp.where(match, logit, 0.0)
        gate = jnp.where(logit >= 0.0, 1.0, small) / (1.0 + small)
        coefficient = (gate - jnp.where(match, 1.0, 0.0)).astype(jnp.bfloat16)
        losses[side] += loss
        total[side] += jnp.dot(coefficient, moving, preferred_element_type=jnp.float32)

    def arrive(slot, piece):
        rows = pl.ds(pl.multiple_of(piece * SEND, SEND), SEND)
        pltpu.make_async_copy(held.at[slot, rows], held.at[slot, rows], recv_sem.at[slot, piece]).wait()

    def arrive_rows(slot, chunk):
        for q in range(ROWS // SEND):
            arrive(slot, chunk * (ROWS // SEND) + q)

    def pass_on(hop, chunk):
        for q in range(ROWS // SEND):
            for down in range(2):
                piece = chunk * (ROWS // SEND) + q
                arrive(7 + 3 * down + hop, piece)
                onward(down, hop, piece).start()

    near = 5 - 3 * odd
    nearby = 8 + jnp.where(mine[0] == 0, 5, 0)

    def labels_arrive(slot):
        pltpu.make_async_copy(labels.at[slot], labels.at[slot], label_recv.at[slot]).wait()

    def rounds(n, carry):
        hop, chunk = n // chunks + 1, lax.rem(n, chunks)
        pass_on(hop, chunk)

        @pl.when(n == chunks)
        def _():
            labels_arrive(near)
            labels_arrive(1)

        @pl.when(n == 2 * chunks)
        def _():
            labels_arrive(4)
            labels_arrive(2 + 3 * odd)

        @pl.when(hop == 2)
        def _():
            arrive_rows(near, chunk)
            arrive_rows(1, chunk)

        @pl.when(hop == 3)
        def _():
            arrive_rows(4, chunk)

        buffer_a = jnp.where(hop == 1, 6, jnp.where(hop == 2, near, 4))
        side_a = jnp.where(hop == 1, 0, jnp.where(hop == 2, 1 - odd, 1))
        buffer_b = jnp.where(hop == 1, 7, jnp.where(hop == 2, 1, nearby))
        side_b = jnp.where(hop == 1, 1, jnp.where(hop == 2, 0, odd))
        slot_b = jnp.where(hop == 3, 2 + 3 * odd, buffer_b)

        def pair(i, carry):
            step(
                jnp.where(i == 0, side_a, side_b), jnp.where(i == 0, buffer_a, buffer_b),
                jnp.where(i == 0, buffer_a, slot_b), chunk,
            )
            return carry

        lax.fori_loop(0, 2, pair, 0)
        return carry

    lax.fori_loop(0, 3 * chunks, rounds, 0)

    def finish(side, chunk):
        slot = 3 * side
        arrive_rows(slot, chunk)
        step(side, slot, slot, chunk)

    def ends(n, carry):
        finish(lax.rem(n, 2), n // 2)
        return carry

    labels_arrive(0)
    labels_arrive(3)
    lax.fori_loop(0, 2 * (chunks - 1), ends, 0)
    for side, out in ((0, image_out), (1, text_out)):
        finish(side, chunks - 1)
        out[...] = (jnp.tile(t, (1, out.shape[1] // ROWS)) * total[side]).astype(jnp.bfloat16)
    for c in range(chunks):
        part = losses[0, c * ROWS : (c + 1) * ROWS]
        loss_ref[c : c + 1, :] = jnp.sum(jnp.transpose(part), axis=0, keepdims=True) * (
            1.0 / (4 * held.shape[1])
        )
    for copy in label_copies:
        copy.wait_send()
    for piece in range(pieces):
        first(0, piece).wait_send()
        first(1, piece).wait_send()
        along(0, piece).wait_send()
        along(1, piece).wait_send()
        beside(piece).wait_send()
        for down in range(2):
            for hop in (1, 2, 3):
                onward(down, hop, piece).wait_send()


def per_device(groups, blocks, images, texts, row_pair_labels, logit_scale_log, logit_bias):
    rows, width = images.shape
    chunks = rows // ROWS
    pieces = rows // SEND
    vmem = pl.BlockSpec(memory_space=pltpu.VMEM)
    hbm = pl.BlockSpec(memory_space=pltpu.HBM)
    loss, image_grad, text_grad = pl.pallas_call(
        functools.partial(kernel, groups, blocks),
        out_shape=(
            jax.ShapeDtypeStruct((chunks, ROWS), jnp.float32),
            jax.ShapeDtypeStruct((rows, width), jnp.bfloat16),
            jax.ShapeDtypeStruct((rows, width), jnp.bfloat16),
        ),
        in_specs=[hbm] * 5,
        out_specs=(vmem, vmem, vmem),
        scratch_shapes=[
            pltpu.VMEM((14, rows, width), jnp.bfloat16),
            pltpu.VMEM((8, chunks, ROWS), jnp.int32),
            pltpu.VMEM((rows, ROWS), jnp.float32),
            pltpu.VMEM((2, rows, width), jnp.float32),
            pltpu.VMEM((2, rows, ROWS), jnp.float32),
            pltpu.SMEM((1,), jnp.float32),
            pltpu.SMEM((1,), jnp.float32),
            pltpu.SemaphoreType.DMA((6,)),
            pltpu.SemaphoreType.DMA((11, pieces)),
            pltpu.SemaphoreType.DMA((14, pieces)),
            pltpu.SemaphoreType.DMA((6,)),
            pltpu.SemaphoreType.DMA((6,)),
            pltpu.SemaphoreType.REGULAR,
        ],
        compiler_params=pltpu.CompilerParams(
            collective_id=0, has_side_effects=True, vmem_limit_bytes=52 << 20
        ),
        cost_estimate=pl.CostEstimate(
            flops=32 * rows * rows * width, bytes_accessed=8 * rows * width, transcendentals=24 * rows * rows
        ),
    )(
        logit_scale_log,
        logit_bias,
        *(
            pltpu.with_memory_space_constraint(a, pltpu.HBM)
            for a in (row_pair_labels.reshape(chunks, ROWS), images, texts)
        ),
    )
    return loss.reshape(rows), image_grad, text_grad


def solution(mesh):
    groups, blocks = mesh.shape["grp"], mesh.shape["blk"]
    both = P(("grp", "blk"))
    wide = P(("grp", "blk"), None)
    return jax.shard_map(
        functools.partial(per_device, groups, blocks),
        mesh=mesh,
        in_specs=(wide, wide, both, P(), P()),
        out_specs=(both, wide, wide),
        check_vma=False,
    )
```

time: 110 us -> 96.4 us (0.88); the launches traced: 108 us -> 96.3 us
  Pallas kernels: 101 us -> 91.9 us
  local copies, waits for them, and re-layouts: 4.39 us -> 2.4 us
    pallas_call x1, Pallas kernels: 101 us -> 91.9 us  [per_device(): pl.pallas_call(functools.partial(kernel, groups, blocks), out_shape=(jax....]
    unnamed x7 -> x3, local copies, waits for them, and re-layouts: 4.39 us -> 2.4 us
where the time goes in v2:
time: 96.4 us; the launch traced here: 96.3 us
  Pallas kernels  91.9 us (95%)
  local copies, waits for them, and re-layouts  2.4 us (2%)
  between operations  1.93 us (2%)
    pallas_call x1, Pallas kernels, per_device(): pl.pallas_call(functools.partial(kernel, groups, blocks), out_shape=(jax....  91.9 us
    unnamed x3, local copies, waits for them, and re-layouts  2.4 us

profile of v2, /device:TPU:1, one launch (start us, length us, event | category | flops | bytes accessed | tf_op | source)
XLA Modules:
  0.0 96.3 jit_solution(269901481415094182)
XLA Ops:
  1.9 91.9 %shard_map.76 = (f32[3,128]{1,0:T(4,128)S(1)}, bf16[384,1152]{1,0:T(8,128)(2,1)S(1)}, bf16[384,1152]{1,0:T(8,128)(2,1)S(1)}) custom-call(f32[1]{0:T(128)S(6)} %copy.11.scale_in, f32[1]{0:T(128)S(6)} %copy.12.bias_in, s32[3,128]{1,0:T(4,128)} %bitcast.3, bf16[384,1152]{1,0:T(8,128)(2,1)} %images_ref.1, bf16[384,1152]{1,0:T(8,128)(2,1)} %texts_ref.1), custom_call_target="tpu_custom_call" | custom-call | flops 5435817984 | bytes 3538944 | tf_op jit(solution)/shard_map/pallas_call | solution.py:287
  93.9 0.6 copy.13
  94.4 0.9 copy.14
  95.3 0.9 copy.15

commit v3 on v2

--- a/solution.py
+++ b/solution.py
@@ -11,11 +11,22 @@
 SEND = 128
 
 
+def pairs(still, moving, still_labels, moving_labels, t, b):
+    logit = t * lax.dot_general(
+        still, moving, (((1,), (1,)), ((), ())), preferred_element_type=jnp.float32
+    ) + b
+    match = still_labels == moving_labels
+    small = jnp.exp(-jnp.abs(logit))
+    loss = jnp.maximum(logit, 0.0) + jnp.log1p(small) - jnp.where(match, logit, 0.0)
+    gate = jnp.where(logit >= 0.0, 1.0, small) / (1.0 + small)
+    return loss, (gate - jnp.where(match, 1.0, 0.0)).astype(jnp.bfloat16)
+
+
 def kernel(
     groups, blocks,
-    scale_in, bias_in, labels_in, images_ref, texts_ref,
-    loss_ref, image_out, text_out,
-    held, labels, columns, total, losses, scale_ref, bias_ref,
+    scale_ref, bias_ref, labels_in, images_ref, texts_ref,
+    total, losses, columns, own, last, marks,
+    held, labels,
     load_sem, send_sem, recv_sem, label_send, label_recv, ready,
 ):
     g, k = lax.axis_index("grp"), lax.axis_index("blk")
@@ -84,15 +95,11 @@
         pltpu.make_async_copy(labels_in, labels.at[6], load_sem.at[2]),
         pltpu.make_async_copy(texts_ref, held.at[6], load_sem.at[0]),
         pltpu.make_async_copy(images_ref, held.at[7], load_sem.at[1]),
-        pltpu.make_async_copy(scale_in, scale_ref, load_sem.at[3]),
-        pltpu.make_async_copy(bias_in, bias_ref, load_sem.at[4]),
-        pltpu.make_async_copy(labels_in, labels.at[7], load_sem.at[5]),
+        pltpu.make_async_copy(labels_in, labels.at[7], load_sem.at[3]),
     ]
     barrier = pltpu.get_barrier_semaphore()
-    for peer in near_z + [partner] + far:
+    for peer in near_z + [partner]:
         pl.semaphore_signal(barrier, inc=1, device_id=peer, device_id_type=MESH)
-    for load in loads:
-        load.start()
 
     @pl.when(odd == 0)
     def _():
@@ -141,6 +148,10 @@
     for piece in range(pieces):
         first(0, piece).start()
         first(1, piece).start()
+    for peer in far:
+        pl.semaphore_signal(barrier, inc=1, device_id=peer, device_id_type=MESH)
+    for load in loads:
+        load.start()
 
     @pl.when(odd == 1)
     def _():
@@ -162,24 +173,24 @@
         beside(piece).start()
 
     t = jnp.exp(jnp.full((1, ROWS), scale_ref[0], jnp.float32))
-    b = bias_ref[0]
+    b = jnp.full((1, ROWS), bias_ref[0], jnp.float32)
     for c in range(chunks):
         row = labels[6, c : c + 1, :].astype(jnp.float32)
         columns[c * ROWS : (c + 1) * ROWS] = jnp.transpose(jnp.broadcast_to(row, (ROWS, ROWS)))
     total[...] = jnp.zeros_like(total)
     losses[...] = jnp.zeros_like(losses)
 
+    marks[0:1] = t
+    marks[1:2] = b
+    for side in range(2):
+        own[side] = held[7 - side]
+
     def step(side, buffer, slot, chunk):
         rows = pl.ds(pl.multiple_of(chunk * ROWS, ROWS), ROWS)
         moving = held[buffer, rows]
-        logit = t * lax.dot_general(
-            held[7 - side], moving, (((1,), (1,)), ((), ())), preferred_element_type=jnp.float32
-        ) + b
-        match = columns[...] == labels[slot, pl.ds(chunk, 1)].astype(jnp.float32)
-        small = jnp.exp(-jnp.abs(logit))
-        loss = jnp.maximum(logit, 0.0) + jnp.log1p(small) - jnp.where(match, logit, 0.0)
-        gate = jnp.where(logit >= 0.0, 1.0, small) / (1.0 + small)
-        coefficient = (gate - jnp.where(match, 1.0, 0.0)).astype(jnp.bfloat16)
+        loss, coefficient = pairs(
+            held[7 - side], moving, columns[...], labels[slot, pl.ds(chunk, 1)].astype(jnp.float32), t, b
+        )
         losses[side] += loss
         total[side] += jnp.dot(coefficient, moving, preferred_element_type=jnp.float32)
 
@@ -257,14 +268,10 @@
     labels_arrive(0)
     labels_arrive(3)
     lax.fori_loop(0, 2 * (chunks - 1), ends, 0)
-    for side, out in ((0, image_out), (1, text_out)):
-        finish(side, chunks - 1)
-        out[...] = (jnp.tile(t, (1, out.shape[1] // ROWS)) * total[side]).astype(jnp.bfloat16)
-    for c in range(chunks):
-        part = losses[0, c * ROWS : (c + 1) * ROWS]
-        loss_ref[c : c + 1, :] = jnp.sum(jnp.transpose(part), axis=0, keepdims=True) * (
-            1.0 / (4 * held.shape[1])
-        )
+    for side in range(2):
+        arrive_rows(3 * side, chunks - 1)
+        last[side] = held[3 * side, (chunks - 1) * ROWS :]
+        marks[2 + side : 3 + side] = labels[3 * side, chunks - 1 :].astype(jnp.float32)
     for copy in label_copies:
         copy.wait_send()
     for piece in range(pieces):
@@ -278,30 +285,61 @@
                 onward(down, hop, piece).wait_send()
 
 
+def finish_kernel(
+    total, losses, columns, own, last, marks,
+    loss_out, image_out, text_out,
+    loss_ref, rounded, sems, loss_sem,
+):
+    chunks = own.shape[1] // ROWS
+    t, b = marks[0:1], marks[1:2]
+    wide_t = jnp.tile(t, (1, own.shape[2] // ROWS))
+    copies = []
+    both_sides = [
+        pairs(own[side], last[side], columns[...], marks[2 + side : 3 + side], t, b) for side in range(2)
+    ]
+    for side, out in ((0, image_out), (1, text_out)):
+        loss_all, coefficient_all = both_sides[side]
+        for c in range(chunks):
+            rows = pl.ds(c * ROWS, ROWS)
+            loss = loss_all[c * ROWS : (c + 1) * ROWS]
+            coefficient = coefficient_all[c * ROWS : (c + 1) * ROWS]
+            grad = total[side, rows] + jnp.dot(coefficient, last[side], preferred_element_type=jnp.float32)
+            rounded[side, rows] = (wide_t * grad).astype(jnp.bfloat16)
+            copies.append(pltpu.make_async_copy(rounded.at[side, rows], out.at[rows], sems.at[side, c]))
+            copies[-1].start()
+            if side == 0:
+                loss_ref[c : c + 1, :] = jnp.sum(
+                    jnp.transpose(losses[0, rows] + loss), axis=0, keepdims=True
+                ) * (1.0 / (4 * own.shape[1]))
+        if side == 0:
+            copies.append(pltpu.make_async_copy(loss_ref, loss_out, loss_sem))
+            copies[-1].start()
+    for copy in copies:
+        copy.wait()
+
+
 def per_device(groups, blocks, images, texts, row_pair_labels, logit_scale_log, logit_bias):
     rows, width = images.shape
     chunks = rows // ROWS
     pieces = rows // SEND
     vmem = pl.BlockSpec(memory_space=pltpu.VMEM)
     hbm = pl.BlockSpec(memory_space=pltpu.HBM)
-    loss, image_grad, text_grad = pl.pallas_call(
+    parts = pl.pallas_call(
         functools.partial(kernel, groups, blocks),
         out_shape=(
-            jax.ShapeDtypeStruct((chunks, ROWS), jnp.float32),
-            jax.ShapeDtypeStruct((rows, width), jnp.bfloat16),
-            jax.ShapeDtypeStruct((rows, width), jnp.bfloat16),
-        ),
-        in_specs=[hbm] * 5,
-        out_specs=(vmem, vmem, vmem),
+            pltpu.VMEM((2, rows, width), jnp.float32),
+            pltpu.VMEM((2, rows, ROWS), jnp.float32),
+            pltpu.VMEM((rows, ROWS), jnp.float32),
+            pltpu.VMEM((2, rows, width), jnp.bfloat16),
+            pltpu.VMEM((2, ROWS, width), jnp.bfloat16),
+            pltpu.VMEM((8, ROWS), jnp.float32),
+        ),
+        in_specs=[pl.BlockSpec(memory_space=pltpu.SMEM)] * 2 + [hbm] * 3,
+        out_specs=(vmem,) * 6,
         scratch_shapes=[
             pltpu.VMEM((14, rows, width), jnp.bfloat16),
             pltpu.VMEM((8, chunks, ROWS), jnp.int32),
-            pltpu.VMEM((rows, ROWS), jnp.float32),
-            pltpu.VMEM((2, rows, width), jnp.float32),
-            pltpu.VMEM((2, rows, ROWS), jnp.float32),
-            pltpu.SMEM((1,), jnp.float32),
-            pltpu.SMEM((1,), jnp.float32),
-            pltpu.SemaphoreType.DMA((6,)),
+            pltpu.SemaphoreType.DMA((4,)),
             pltpu.SemaphoreType.DMA((11, pieces)),
             pltpu.SemaphoreType.DMA((14, pieces)),
             pltpu.SemaphoreType.DMA((6,)),
@@ -309,7 +347,7 @@
             pltpu.SemaphoreType.REGULAR,
         ],
         compiler_params=pltpu.CompilerParams(
-            collective_id=0, has_side_effects=True, vmem_limit_bytes=52 << 20
+            collective_id=0, has_side_effects=True, vmem_limit_bytes=40 << 20
         ),
         cost_estimate=pl.CostEstimate(
             flops=32 * rows * rows * width, bytes_accessed=8 * rows * width, transcendentals=24 * rows * rows
@@ -322,6 +360,23 @@
             for a in (row_pair_labels.reshape(chunks, ROWS), images, texts)
         ),
     )
+    loss, image_grad, text_grad = pl.pallas_call(
+        finish_kernel,
+        out_shape=(
+            jax.ShapeDtypeStruct((chunks, ROWS), jnp.float32),
+            jax.ShapeDtypeStruct((rows, width), jnp.bfloat16),
+            jax.ShapeDtypeStruct((rows, width), jnp.bfloat16),
+        ),
+        in_specs=[vmem] * 6,
+        out_specs=(hbm,) * 3,
+        scratch_shapes=[
+            pltpu.VMEM((chunks, ROWS), jnp.float32),
+            pltpu.VMEM((2, rows, width), jnp.bfloat16),
+            pltpu.SemaphoreType.DMA((2, chunks)),
+            pltpu.SemaphoreType.DMA,
+        ],
+        compiler_params=pltpu.CompilerParams(vmem_limit_bytes=24 << 20),
+    )(*(pltpu.with_memory_space_constraint(a, pltpu.VMEM) for a in parts))
     return loss.reshape(rows), image_grad, text_grad
 
 

time: 96.4 us -> 94 us (0.975)
  local copies, waits for them, and re-layouts: 2.4 us -> 0 us
    unnamed x3 -> x0, local copies, waits for them, and re-layouts: 2.4 us -> none
    pallas_call x1 -> x2, Pallas kernels: 91.9 us -> 91.9 us  [the longest x1 89.8 us: per_device(): pl.pallas_call(functools.partial(kernel, groups, blocks), out_shape=(pltp...]
where the time goes in v3:
time: 94 us; the launch traced here: 93.8 us
  Pallas kernels  91.9 us (98%)
  between operations  1.93 us (2%)
    pallas_call x1, Pallas kernels, per_device(): pl.pallas_call(functools.partial(kernel, groups, blocks), out_shape=(pltp...  89.8 us
    pallas_call x1, Pallas kernels, per_device(): pl.pallas_call(finish_kernel, out_shape=(jax.ShapeDtypeStruct((chunks, RO...  2.11 us

profile of v3, /device:TPU:1, one launch (start us, length us, event | category | flops | bytes accessed | tf_op | source)
XLA Modules:
  0.0 93.8 jit_solution(16500326984779906588)
XLA Ops:
  1.9 89.8 %shard_map.76 = (f32[2,384,1152]{2,1,0:T(8,128)S(1)}, f32[2,384,128]{2,1,0:T(8,128)S(1)}, f32[384,128]{1,0:T(8,128)S(1)}, bf16[2,384,1152]{2,1,0:T(8,128)(2,1)S(...) custom-call(f32[1]{0:T(128)S(6)} %copy.8.scale_ref, f32[1]{0:T(128)S(6)} %copy.9.bias_ref, s32[3,128]{1,0:T(4,128)} %bitcast.2, ...), custom_call_target="tpu_custom_call" | custom-call | flops 5435817984 | bytes 3538944 | tf_op jit(solution)/shard_map/pallas_call | solution.py:327
  91.7 2.1 %shard_map.77 = (f32[3,128]{1,0:T(4,128)}, bf16[384,1152]{1,0:T(8,128)(2,1)}, bf16[384,1152]{1,0:T(8,128)(2,1)}) custom-call(f32[2,384,1152]{2,1,0:T(8,128)S(1)} %get-tuple-element.12.total, f32[2,384,128]{2,1,0:T(8,128)S(1)} %get-tuple-element.13.losses, f32[384,128]{1,0:T(8,128)S(1)} %get-tuple-element.14.columns, ...), custom_call_target="tpu_custom_call" | custom-call | tf_op jit(solution)/shard_map/pallas_call | solution.py:363

commit v4 on v3

--- a/solution.py
+++ b/solution.py
@@ -8,7 +8,7 @@
 
 MESH = pl.DeviceIdType.MESH
 ROWS = 128
-SEND = 128
+SPLIT = 32
 
 
 def pairs(still, moving, still_labels, moving_labels, t, b):
@@ -32,7 +32,6 @@
     g, k = lax.axis_index("grp"), lax.axis_index("blk")
     odd = lax.rem(g, 2)
     chunks = held.shape[1] // ROWS
-    pieces = held.shape[1] // SEND
     lows = groups // 2
     deep = 2 * lows
 
@@ -48,6 +47,26 @@
     def on_chip(z, core, place):
         z = lax.rem(z + 2 * deep, deep)
         return (2 * lax.rem(z, lows) + core, place[1] - lax.rem(place[1], 2) + z // lows)
+
+    z_here = height((g, k))
+    near_z = [on_chip(z_here + 1, 0, (g, k)), on_chip(z_here - 1, 0, (g, k))]
+    partner = (g + 1 - 2 * odd, k)
+    barrier = pltpu.get_barrier_semaphore()
+    for peer in near_z + [partner]:
+        pl.semaphore_signal(barrier, inc=1, device_id=peer, device_id_type=MESH)
+    block_loads = [
+        [
+            pltpu.make_async_copy(
+                source.at[pl.ds(chunk * ROWS, ROWS)], held.at[slot, pl.ds(chunk * ROWS, ROWS)],
+                load_sem.at[4 + 2 * chunk + slot - 6],
+            )
+            for source, slot in ((texts_ref, 6), (images_ref, 7))
+        ]
+        for chunk in range(chunks)
+    ]
+    for pair in block_loads:
+        for load in pair:
+            load.start()
 
     def inner(z):
         return jnp.where(lax.rem(z + 2 * deep, lows) < lows - 1, 1, 0)
@@ -84,23 +103,14 @@
     targets = [at(0, 1), at(0, 2), at(1, 0), at(0, -1), at(0, -2), at(-1, 0)]
     text_first, text_down = first_to(0)
     image_first, image_down = first_to(1)
-    z_here = height((g, k))
     low = g // 2
-    near_z = [on_chip(z_here + 1, 0, (g, k)), on_chip(z_here - 1, 0, (g, k))]
     far = [
         moved(on_chip(z_here + up, 1, (g, k)), side) for side in (-1, 1) for up in (-1, 0, 1)
     ] + [(2 * low + 1, at(0, 1)[1]), (2 * low + 1, at(0, -1)[1]), (2 * (lows - 1 - low) + 1, k)]
-    partner = (g + 1 - 2 * odd, k)
     loads = [
         pltpu.make_async_copy(labels_in, labels.at[6], load_sem.at[2]),
-        pltpu.make_async_copy(texts_ref, held.at[6], load_sem.at[0]),
-        pltpu.make_async_copy(images_ref, held.at[7], load_sem.at[1]),
         pltpu.make_async_copy(labels_in, labels.at[7], load_sem.at[3]),
     ]
-    barrier = pltpu.get_barrier_semaphore()
-    for peer in near_z + [partner]:
-        pl.semaphore_signal(barrier, inc=1, device_id=peer, device_id_type=MESH)
-
     @pl.when(odd == 0)
     def _():
         pl.semaphore_wait(barrier, 2 * len(near_z) + 1)
@@ -110,31 +120,65 @@
     def _():
         pl.semaphore_wait(ready, 1)
 
+    tail = chunks * ROWS - SPLIT
+
+    def rows_of(piece):
+        if isinstance(piece, int) and piece >= chunks - 1:
+            return pl.ds(tail, SPLIT) if piece == chunks else pl.ds((chunks - 1) * ROWS, ROWS - SPLIT)
+        return pl.ds(pl.multiple_of(piece * ROWS, ROWS), ROWS)
+
     def block_copy(source, slot, piece, flow, device):
-        rows = pl.ds(pl.multiple_of(piece * SEND, SEND), SEND)
+        rows = rows_of(piece)
         return pltpu.make_async_remote_copy(
             src_ref=source.at[rows], dst_ref=held.at[slot, rows],
             send_sem=send_sem.at[flow, piece], recv_sem=recv_sem.at[slot, piece],
             device_id=device, device_id_type=MESH,
         )
 
+    def whole_copy(source, slot, chunk, flow, device):
+        rows = pl.ds(chunk * ROWS, ROWS)
+        return pltpu.make_async_remote_copy(
+            src_ref=source.at[rows], dst_ref=held.at[slot, rows],
+            send_sem=send_sem.at[flow, chunk], recv_sem=recv_sem.at[slot, chunk],
+            device_id=device, device_id_type=MESH,
+        )
+
+    top = deep - 1
+    down_to = world(
+        odd,
+        moved(
+            on_chip(z + 2 * odd - 1, 0, mine), jnp.where(z_here == lows, 1 - odd, 0)
+        ),
+    )
+
     def first(w, piece):
+        source, down, device = [(6, text_down, text_first), (7, image_down, image_first)][w]
+        slot = 8 + 3 * down
+        if piece == chunks:
+            turned = jnp.where(odd == w, jnp.where(z_here == top, 1, 0), 0)
+            slot = jnp.where(turned == 1, 14, slot)
+            device = tuple(jnp.where(turned == 1, x, y) for x, y in zip(down_to, device))
+        return block_copy(held.at[source], slot, piece, w, device)
+
+    def short_down():
+        slot = jnp.where(z_here == lows, 3 * odd, 14)
+        return block_copy(held.at[14], slot, chunks, 11, down_to)
+
+    def along(w, chunk):
         if w == 0:
-            return block_copy(texts_ref, 8 + 3 * text_down, piece, 0, text_first)
-        return block_copy(images_ref, 8 + 3 * image_down, piece, 1, image_first)
-
-    def along(w, piece):
-        if w == 0:
-            return block_copy(texts_ref, 1, piece, 2, targets[1])
-        return block_copy(images_ref, 4, piece, 3, targets[4])
-
-    def beside(piece):
-        return block_copy(held.at[6 + odd], 2 + 3 * odd, piece, 4, partner)
+            return whole_copy(held.at[6], 1, chunk, 2, targets[1])
+        return whole_copy(held.at[7], 4, chunk, 3, targets[4])
+
+    def beside(chunk):
+        return whole_copy(held.at[6 + odd], 2 + 3 * odd, chunk, 4, partner)
 
     def onward(down, hop, piece):
         buffer = 7 + 3 * down + hop
         slot = jnp.where(hop == 3, 3 * odd, buffer + 1)
         return block_copy(held.at[buffer], slot, piece, 4 + 3 * down + hop, goes_to(down, hop))
+
+    def is_short(down, hop):
+        return jnp.where(odd == down, jnp.where(hop == z_here + 1, 1, 0), 0)
 
     label_copies = [
         pltpu.make_async_remote_copy(
@@ -145,9 +189,13 @@
         for slot in range(6)
     ]
 
-    for piece in range(pieces):
-        first(0, piece).start()
-        first(1, piece).start()
+    for chunk in range(chunks):
+        for load in block_loads[chunk]:
+            load.wait()
+        first(0, chunk).start()
+        first(1, chunk).start()
+    first(0, chunks).start()
+    first(1, chunks).start()
     for peer in far:
         pl.semaphore_signal(barrier, inc=1, device_id=peer, device_id_type=MESH)
     for load in loads:
@@ -164,13 +212,13 @@
 
     for copy in label_copies:
         copy.start()
-    for piece in range(pieces):
-        along(0, piece).start()
-        along(1, piece).start()
+    for chunk in range(chunks):
+        along(0, chunk).start()
+        along(1, chunk).start()
     for load in loads:
         load.wait()
-    for piece in range(pieces):
-        beside(piece).start()
+    for chunk in range(chunks):
+        beside(chunk).start()
 
     t = jnp.exp(jnp.full((1, ROWS), scale_ref[0], jnp.float32))
     b = jnp.full((1, ROWS), bias_ref[0], jnp.float32)
@@ -195,19 +243,33 @@
         total[side] += jnp.dot(coefficient, moving, preferred_element_type=jnp.float32)
 
     def arrive(slot, piece):
-        rows = pl.ds(pl.multiple_of(piece * SEND, SEND), SEND)
+        rows = rows_of(piece)
         pltpu.make_async_copy(held.at[slot, rows], held.at[slot, rows], recv_sem.at[slot, piece]).wait()
 
     def arrive_rows(slot, chunk):
-        for q in range(ROWS // SEND):
-            arrive(slot, chunk * (ROWS // SEND) + q)
+        rows = pl.ds(pl.multiple_of(chunk * ROWS, ROWS), ROWS)
+        pltpu.make_async_copy(held.at[slot, rows], held.at[slot, rows], recv_sem.at[slot, chunk]).wait()
 
     def pass_on(hop, chunk):
-        for q in range(ROWS // SEND):
-            for down in range(2):
-                piece = chunk * (ROWS // SEND) + q
-                arrive(7 + 3 * down + hop, piece)
-                onward(down, hop, piece).start()
+        for down in range(2):
+            @pl.when(chunk < chunks - 1)
+            def _():
+                arrive(7 + 3 * down + hop, chunk)
+                onward(down, hop, chunk).start()
+
+            @pl.when(chunk == chunks - 1)
+            def _():
+                arrive(7 + 3 * down + hop, chunks - 1)
+                onward(down, hop, chunks - 1).start()
+
+                @pl.when(is_short(down, hop) == 0)
+                def _():
+                    arrive(7 + 3 * down + hop, chunks)
+                    onward(down, hop, chunks).start()
+
+    turned_at = jnp.where(
+        z_here == top - 1, chunks, jnp.where(z_here == top - 2, 2 * chunks, jnp.where(z_here == lows, 3 * chunks - 1, -1))
+    )
 
     near = 5 - 3 * odd
     nearby = 8 + jnp.where(mine[0] == 0, 5, 0)
@@ -218,6 +280,11 @@
     def rounds(n, carry):
         hop, chunk = n // chunks + 1, lax.rem(n, chunks)
         pass_on(hop, chunk)
+
+        @pl.when(n == turned_at)
+        def _():
+            arrive(14, chunks)
+            short_down().start()
 
         @pl.when(n == chunks)
         def _():
@@ -256,33 +323,47 @@
 
     lax.fori_loop(0, 3 * chunks, rounds, 0)
 
-    def finish(side, chunk):
-        slot = 3 * side
-        arrive_rows(slot, chunk)
-        step(side, slot, slot, chunk)
-
-    def ends(n, carry):
-        finish(lax.rem(n, 2), n // 2)
-        return carry
-
+    for copy in label_copies:
+        copy.wait_send()
+    for chunk in range(chunks):
+        along(0, chunk).wait_send()
+        along(1, chunk).wait_send()
+        beside(chunk).wait_send()
+    for piece in range(chunks + 1):
+        first(0, piece).wait_send()
+        first(1, piece).wait_send()
+
+    def sent(hop):
+        for down in range(2):
+            for piece in range(chunks):
+                onward(down, hop, piece).wait_send()
+
+            @pl.when(is_short(down, hop) == 0)
+            def _():
+                onward(down, hop, chunks).wait_send()
+
+    sent(1)
+    sent(2)
     labels_arrive(0)
     labels_arrive(3)
+
+    def ends(n, carry):
+        side, chunk = lax.rem(n, 2), n // 2
+        arrive_rows(3 * side, chunk)
+        step(side, 3 * side, 3 * side, chunk)
+        return carry
+
     lax.fori_loop(0, 2 * (chunks - 1), ends, 0)
     for side in range(2):
-        arrive_rows(3 * side, chunks - 1)
+        arrive(3 * side, chunks - 1)
+        arrive(3 * side, chunks)
         last[side] = held[3 * side, (chunks - 1) * ROWS :]
         marks[2 + side : 3 + side] = labels[3 * side, chunks - 1 :].astype(jnp.float32)
-    for copy in label_copies:
-        copy.wait_send()
-    for piece in range(pieces):
-        first(0, piece).wait_send()
-        first(1, piece).wait_send()
-        along(0, piece).wait_send()
-        along(1, piece).wait_send()
-        beside(piece).wait_send()
-        for down in range(2):
-            for hop in (1, 2, 3):
-                onward(down, hop, piece).wait_send()
+    sent(3)
+
+    @pl.when(turned_at >= 0)
+    def _():
+        short_down().wait_send()
 
 
 def finish_kernel(
@@ -321,7 +402,7 @@
 def per_device(groups, blocks, images, texts, row_pair_labels, logit_scale_log, logit_bias):
     rows, width = images.shape
     chunks = rows // ROWS
-    pieces = rows // SEND
+    pieces = chunks + 1
     vmem = pl.BlockSpec(memory_space=pltpu.VMEM)
     hbm = pl.BlockSpec(memory_space=pltpu.HBM)
     parts = pl.pallas_call(
@@ -337,11 +418,11 @@
         in_specs=[pl.BlockSpec(memory_space=pltpu.SMEM)] * 2 + [hbm] * 3,
         out_specs=(vmem,) * 6,
         scratch_shapes=[
-            pltpu.VMEM((14, rows, width), jnp.bfloat16),
+            pltpu.VMEM((15, rows, width), jnp.bfloat16),
             pltpu.VMEM((8, chunks, ROWS), jnp.int32),
-            pltpu.SemaphoreType.DMA((4,)),
-            pltpu.SemaphoreType.DMA((11, pieces)),
-            pltpu.SemaphoreType.DMA((14, pieces)),
+            pltpu.SemaphoreType.DMA((4 + 2 * chunks,)),
+            pltpu.SemaphoreType.DMA((12, pieces)),
+            pltpu.SemaphoreType.DMA((15, pieces)),
             pltpu.SemaphoreType.DMA((6,)),
             pltpu.SemaphoreType.DMA((6,)),
             pltpu.SemaphoreType.REGULAR,

time: 94 us -> 92.3 us (0.982)
  Pallas kernels: 91.9 us -> 90.2 us
    pallas_call x1, Pallas kernels: 89.8 us -> 88.1 us  [per_device(): pl.pallas_call(functools.partial(kernel, groups, blocks), out_shape=(pltp...]
where the time goes in v4:
time: 92.3 us; the launch traced here: 92.2 us
  Pallas kernels  90.2 us (98%)
  between operations  1.93 us (2%)
    pallas_call x1, Pallas kernels, per_device(): pl.pallas_call(functools.partial(kernel, groups, blocks), out_shape=(pltp...  88.1 us
    pallas_call x1, Pallas kernels, per_device(): pl.pallas_call(finish_kernel, out_shape=(jax.ShapeDtypeStruct((chunks, RO...  2.11 us

profile of v4, /device:TPU:1, one launch (start us, length us, event | category | flops | bytes accessed | tf_op | source)
XLA Modules:
  0.0 92.2 jit_solution(16706995288803513560)
XLA Ops:
  1.9 88.1 %shard_map.76 = (f32[2,384,1152]{2,1,0:T(8,128)S(1)}, f32[2,384,128]{2,1,0:T(8,128)S(1)}, f32[384,128]{1,0:T(8,128)S(1)}, bf16[2,384,1152]{2,1,0:T(8,128)(2,1)S(...) custom-call(f32[1]{0:T(128)S(6)} %copy.8.scale_ref, f32[1]{0:T(128)S(6)} %copy.9.bias_ref, s32[3,128]{1,0:T(4,128)} %bitcast.2, ...), custom_call_target="tpu_custom_call" | custom-call | flops 5435817984 | bytes 3538944 | tf_op jit(solution)/shard_map/pallas_call | solution.py:408
  90.1 2.1 %shard_map.77 = (f32[3,128]{1,0:T(4,128)}, bf16[384,1152]{1,0:T(8,128)(2,1)}, bf16[384,1152]{1,0:T(8,128)(2,1)}) custom-call(f32[2,384,1152]{2,1,0:T(8,128)S(1)} %get-tuple-element.12.total, f32[2,384,128]{2,1,0:T(8,128)S(1)} %get-tuple-element.13.losses, f32[384,128]{1,0:T(8,128)S(1)} %get-tuple-element.14.columns, ...), custom_call_target="tpu_custom_call" | custom-call | tf_op jit(solution)/shard_map/pallas_call | solution.py:444

commit v5 on v4

--- a/solution.py
+++ b/solution.py
@@ -8,7 +8,7 @@
 
 MESH = pl.DeviceIdType.MESH
 ROWS = 128
-SPLIT = 32
+SPLIT = 64
 
 
 def pairs(still, moving, still_labels, moving_labels, t, b):
@@ -27,7 +27,7 @@
     scale_ref, bias_ref, labels_in, images_ref, texts_ref,
     total, losses, columns, own, last, marks,
     held, labels,
-    load_sem, send_sem, recv_sem, label_send, label_recv, ready,
+    load_sem, send_sem, recv_sem, label_send, label_recv, ready, up_ready,
 ):
     g, k = lax.axis_index("grp"), lax.axis_index("blk")
     odd = lax.rem(g, 2)
@@ -49,11 +49,16 @@
         return (2 * lax.rem(z, lows) + core, place[1] - lax.rem(place[1], 2) + z // lows)
 
     z_here = height((g, k))
-    near_z = [on_chip(z_here + 1, 0, (g, k)), on_chip(z_here - 1, 0, (g, k))]
+    top = deep - 1
     partner = (g + 1 - 2 * odd, k)
     barrier = pltpu.get_barrier_semaphore()
-    for peer in near_z + [partner]:
+    for peer in (on_chip(z_here + 1, 0, (g, k)), partner):
         pl.semaphore_signal(barrier, inc=1, device_id=peer, device_id_type=MESH)
+
+    @pl.when(z_here == 0)
+    def _():
+        pl.semaphore_signal(barrier, inc=1, device_id=on_chip(z_here - 1, 0, (g, k)), device_id_type=MESH)
+
     block_loads = [
         [
             pltpu.make_async_copy(
@@ -111,14 +116,26 @@
         pltpu.make_async_copy(labels_in, labels.at[6], load_sem.at[2]),
         pltpu.make_async_copy(labels_in, labels.at[7], load_sem.at[3]),
     ]
-    @pl.when(odd == 0)
-    def _():
-        pl.semaphore_wait(barrier, 2 * len(near_z) + 1)
-        pl.semaphore_signal(ready, inc=1, device_id=partner, device_id_type=MESH)
-
-    @pl.when(odd == 1)
-    def _():
-        pl.semaphore_wait(ready, 1)
+    def wait_below():
+        @pl.when(odd == 0)
+        def _():
+            pl.semaphore_wait(barrier, jnp.where(z_here == top, 5, 3))
+            pl.semaphore_signal(ready, inc=1, device_id=partner, device_id_type=MESH)
+
+            @pl.when(z_here > 0)
+            def _():
+                for core in range(2):
+                    below = on_chip(z_here - 1, core, (g, k))
+                    pl.semaphore_signal(up_ready, inc=1, device_id=below, device_id_type=MESH)
+
+        @pl.when(odd == 1)
+        def _():
+            pl.semaphore_wait(ready, 1)
+
+    def wait_above():
+        @pl.when(z_here < top)
+        def _():
+            pl.semaphore_wait(up_ready, 1)
 
     tail = chunks * ROWS - SPLIT
 
@@ -143,26 +160,23 @@
             device_id=device, device_id_type=MESH,
         )
 
-    top = deep - 1
-    down_to = world(
-        odd,
-        moved(
-            on_chip(z + 2 * odd - 1, 0, mine), jnp.where(z_here == lows, 1 - odd, 0)
-        ),
-    )
+    rising = jnp.where(z_here < lows, 1, 0)
+    passed = jnp.where(rising == 1, z_here, top - z_here)
+    turns_now = jnp.where(passed == lows - 1, jnp.where(rising == 1, odd, 1 - odd), 0)
+    turned_to = world(odd, moved(on_chip(z + (2 * rising - 1) * (1 - 2 * odd), 0, mine), turns_now))
 
     def first(w, piece):
         source, down, device = [(6, text_down, text_first), (7, image_down, image_first)][w]
         slot = 8 + 3 * down
         if piece == chunks:
-            turned = jnp.where(odd == w, jnp.where(z_here == top, 1, 0), 0)
+            turned = jnp.where(odd == w, jnp.where(passed == 0, 1, 0), 0)
             slot = jnp.where(turned == 1, 14, slot)
-            device = tuple(jnp.where(turned == 1, x, y) for x, y in zip(down_to, device))
+            device = tuple(jnp.where(turned == 1, x, y) for x, y in zip(turned_to, device))
         return block_copy(held.at[source], slot, piece, w, device)
 
-    def short_down():
-        slot = jnp.where(z_here == lows, 3 * odd, 14)
-        return block_copy(held.at[14], slot, chunks, 11, down_to)
+    def turned_on():
+        slot = jnp.where(passed == lows - 1, 3 * odd, 14)
+        return block_copy(held.at[14], slot, chunks, 11, turned_to)
 
     def along(w, chunk):
         if w == 0:
@@ -178,7 +192,7 @@
         return block_copy(held.at[buffer], slot, piece, 4 + 3 * down + hop, goes_to(down, hop))
 
     def is_short(down, hop):
-        return jnp.where(odd == down, jnp.where(hop == z_here + 1, 1, 0), 0)
+        return jnp.where(hop == jnp.where(odd == down, z_here + 1, deep - z_here), 1, 0)
 
     label_copies = [
         pltpu.make_async_remote_copy(
@@ -189,13 +203,22 @@
         for slot in range(6)
     ]
 
-    for chunk in range(chunks):
-        for load in block_loads[chunk]:
-            load.wait()
-        first(0, chunk).start()
-        first(1, chunk).start()
-    first(0, chunks).start()
-    first(1, chunks).start()
+    def send_first(falling):
+        for w, falls in ((0, text_down), (1, 1 - image_down)):
+            @pl.when(falls == falling)
+            def _():
+                for chunk in range(chunks):
+                    block_loads[chunk][w].wait()
+                    first(w, chunk).start()
+                first(w, chunks).start()
+
+    lowest = jnp.where(z_here == 0, 1, 0)
+    pl.when(lowest == 0)(wait_below)
+    pl.when(lowest == 1)(wait_above)
+    send_first(1 - lowest)
+    pl.when(lowest == 0)(wait_above)
+    pl.when(lowest == 1)(wait_below)
+    send_first(lowest)
     for peer in far:
         pl.semaphore_signal(barrier, inc=1, device_id=peer, device_id_type=MESH)
     for load in loads:
@@ -268,7 +291,7 @@
                     onward(down, hop, chunks).start()
 
     turned_at = jnp.where(
-        z_here == top - 1, chunks, jnp.where(z_here == top - 2, 2 * chunks, jnp.where(z_here == lows, 3 * chunks - 1, -1))
+        passed == 1, chunks, jnp.where(passed == 2, 2 * chunks, jnp.where(passed == 3, 3 * chunks - 1, -1))
     )
 
     near = 5 - 3 * odd
@@ -284,7 +307,7 @@
         @pl.when(n == turned_at)
         def _():
             arrive(14, chunks)
-            short_down().start()
+            turned_on().start()
 
         @pl.when(n == chunks)
         def _():
@@ -363,7 +386,7 @@
 
     @pl.when(turned_at >= 0)
     def _():
-        short_down().wait_send()
+        turned_on().wait_send()
 
 
 def finish_kernel(
@@ -425,6 +448,7 @@
             pltpu.SemaphoreType.DMA((15, pieces)),
             pltpu.SemaphoreType.DMA((6,)),
             pltpu.SemaphoreType.DMA((6,)),
+            pltpu.SemaphoreType.REGULAR,
             pltpu.SemaphoreType.REGULAR,
         ],
         compiler_params=pltpu.CompilerParams(

time: 92.3 us -> 90.9 us (0.985)
  Pallas kernels: 90.2 us -> 88.6 us
    pallas_call x1, Pallas kernels: 88.1 us -> 86.5 us  [per_device(): pl.pallas_call(functools.partial(kernel, groups, blocks), out_shape=(pltp...]
where the time goes in v5:
time: 90.9 us; the launch traced here: 90.5 us
  Pallas kernels  88.6 us (97%)
  between operations  1.93 us (2%)
    pallas_call x1, Pallas kernels, per_device(): pl.pallas_call(functools.partial(kernel, groups, blocks), out_shape=(pltp...  86.5 us
    pallas_call x1, Pallas kernels, per_device(): pl.pallas_call(finish_kernel, out_shape=(jax.ShapeDtypeStruct((chunks, RO...  2.11 us

profile of v5, /device:TPU:1, one launch (start us, length us, event | category | flops | bytes accessed | tf_op | source)
XLA Modules:
  0.0 90.5 jit_solution(7995366871058795423)
XLA Ops:
  1.9 86.5 %shard_map.76 = (f32[2,384,1152]{2,1,0:T(8,128)S(1)}, f32[2,384,128]{2,1,0:T(8,128)S(1)}, f32[384,128]{1,0:T(8,128)S(1)}, bf16[2,384,1152]{2,1,0:T(8,128)(2,1)S(...) custom-call(f32[1]{0:T(128)S(6)} %copy.8.scale_ref, f32[1]{0:T(128)S(6)} %copy.9.bias_ref, s32[3,128]{1,0:T(4,128)} %bitcast.2, ...), custom_call_target="tpu_custom_call" | custom-call | flops 5435817984 | bytes 3538944 | tf_op jit(solution)/shard_map/pallas_call | solution.py:431
  88.4 2.1 %shard_map.77 = (f32[3,128]{1,0:T(4,128)}, bf16[384,1152]{1,0:T(8,128)(2,1)}, bf16[384,1152]{1,0:T(8,128)(2,1)}) custom-call(f32[2,384,1152]{2,1,0:T(8,128)S(1)} %get-tuple-element.12.total, f32[2,384,128]{2,1,0:T(8,128)S(1)} %get-tuple-element.13.losses, f32[384,128]{1,0:T(8,128)S(1)} %get-tuple-element.14.columns, ...), custom_call_target="tpu_custom_call" | custom-call | tf_op jit(solution)/shard_map/pallas_call | solution.py:468

commit v6 on v5

--- a/solution.py
+++ b/solution.py
@@ -8,7 +8,7 @@
 
 MESH = pl.DeviceIdType.MESH
 ROWS = 128
-SPLIT = 64
+SPLIT = 48
 
 
 def pairs(still, moving, still_labels, moving_labels, t, b):
@@ -90,9 +90,8 @@
 
     def turns(down, hop, source):
         source = lax.rem(source + 2 * deep, deep)
-        if down == 0:
-            return jnp.where(hop == 1, source // lows, 0)
-        return jnp.where(hop == 3 - inner(source), source // lows, 0)
+        at_hop = jnp.where(down == 0, 1, 3 - inner(source))
+        return jnp.where(hop == at_hop, source // lows, 0)
 
     def goes_to(down, hop):
         up = 1 - 2 * down
@@ -273,22 +272,25 @@
         rows = pl.ds(pl.multiple_of(chunk * ROWS, ROWS), ROWS)
         pltpu.make_async_copy(held.at[slot, rows], held.at[slot, rows], recv_sem.at[slot, chunk]).wait()
 
-    def pass_on(hop, chunk):
-        for down in range(2):
-            @pl.when(chunk < chunks - 1)
+    early = jnp.where(z_here < lows - 1, 1 - odd, odd)
+
+    def pass_on(down, n):
+        hop, chunk = n // chunks + 1, lax.rem(n, chunks)
+
+        @pl.when(chunk < chunks - 1)
+        def _():
+            arrive(7 + 3 * down + hop, chunk)
+            onward(down, hop, chunk).start()
+
+        @pl.when(chunk == chunks - 1)
+        def _():
+            arrive(7 + 3 * down + hop, chunks - 1)
+            onward(down, hop, chunks - 1).start()
+
+            @pl.when(is_short(down, hop) == 0)
             def _():
-                arrive(7 + 3 * down + hop, chunk)
-                onward(down, hop, chunk).start()
-
-            @pl.when(chunk == chunks - 1)
-            def _():
-                arrive(7 + 3 * down + hop, chunks - 1)
-                onward(down, hop, chunks - 1).start()
-
-                @pl.when(is_short(down, hop) == 0)
-                def _():
-                    arrive(7 + 3 * down + hop, chunks)
-                    onward(down, hop, chunks).start()
+                arrive(7 + 3 * down + hop, chunks)
+                onward(down, hop, chunks).start()
 
     turned_at = jnp.where(
         passed == 1, chunks, jnp.where(passed == 2, 2 * chunks, jnp.where(passed == 3, 3 * chunks - 1, -1))
@@ -302,7 +304,11 @@
 
     def rounds(n, carry):
         hop, chunk = n // chunks + 1, lax.rem(n, chunks)
-        pass_on(hop, chunk)
+        pass_on(1 - early, n)
+
+        @pl.when(n < 3 * chunks - 1)
+        def _():
+            pass_on(early, n + 1)
 
         @pl.when(n == turned_at)
         def _():
@@ -344,6 +350,7 @@
         lax.fori_loop(0, 2, pair, 0)
         return carry
 
+    pass_on(early, 0)
     lax.fori_loop(0, 3 * chunks, rounds, 0)
 
     for copy in label_copies:

time: 90.9 us -> 92 us (1.012); the launches traced: 90.5 us -> 90.5 us
  no operation moved by 1% of the time
where the time goes in v6:
time: 92 us; the launch traced here: 90.5 us
  Pallas kernels  88.6 us (96%)
  between operations  1.93 us (2%)
    pallas_call x1, Pallas kernels, per_device(): pl.pallas_call(functools.partial(kernel, groups, blocks), out_shape=(pltp...  86.5 us
    pallas_call x1, Pallas kernels, per_device(): pl.pallas_call(finish_kernel, out_shape=(jax.ShapeDtypeStruct((chunks, RO...  2.11 us

profile of v6, /device:TPU:1, one launch (start us, length us, event | category | flops | bytes accessed | tf_op | source)
XLA Modules:
  0.0 90.5 jit_solution(4221399153487008941)
XLA Ops:
  1.9 86.5 %shard_map.76 = (f32[2,384,1152]{2,1,0:T(8,128)S(1)}, f32[2,384,128]{2,1,0:T(8,128)S(1)}, f32[384,128]{1,0:T(8,128)S(1)}, bf16[2,384,1152]{2,1,0:T(8,128)(2,1)S(...) custom-call(f32[1]{0:T(128)S(6)} %copy.8.scale_ref, f32[1]{0:T(128)S(6)} %copy.9.bias_ref, s32[3,128]{1,0:T(4,128)} %bitcast.2, ...), custom_call_target="tpu_custom_call" | custom-call | flops 5435817984 | bytes 3538944 | tf_op jit(solution)/shard_map/pallas_call | solution.py:438
  88.4 2.1 %shard_map.77 = (f32[3,128]{1,0:T(4,128)}, bf16[384,1152]{1,0:T(8,128)(2,1)}, bf16[384,1152]{1,0:T(8,128)(2,1)}) custom-call(f32[2,384,1152]{2,1,0:T(8,128)S(1)} %get-tuple-element.12.total, f32[2,384,128]{2,1,0:T(8,128)S(1)} %get-tuple-element.13.losses, f32[384,128]{1,0:T(8,128)S(1)} %get-tuple-element.14.columns, ...), custom_call_target="tpu_custom_call" | custom-call | tf_op jit(solution)/shard_map/pallas_call | solution.py:475
